TPU v7x, 256 devices: a whole 4x4x8 slice. The times are simulated.
256 devices in a mesh: dp: 16 (over y, x), ctx: 16 (over z, core).
Axes of the slice: x: 4, y: 4, z: 8, core: 2. Of those that a mesh axis runs over, the one named last changes fastest.
Arguments:
- frames: bfloat16 [8192, 6144], P('ctx'), may hold values from -6 to 6
- proj_weight: bfloat16 [3, 6144, 4096], P(None, 'ctx', 'dp'), may hold values from -0.078125 to 0.078125
- out_weight: bfloat16 [6144, 4096], P('dp', 'ctx'), may hold values from -0.09375 to 0.09375
- query_gain: float32 [4096], P('dp'), may hold values from 0.5 to 2
- key_gain: float32 [4096], P('dp'), may hold values from 0.5 to 2
- key_tiles: int32 [32, 128, 18], P('dp', 'ctx'), may hold values from 0 to 127, as said below
- key_counts: int32 [32, 128], P('dp', 'ctx'), may hold values from 1 to 18
Outputs:
- mixed: bfloat16 [8192, 6144], P('ctx', 'dp')
Inputs may be any that keep to these rules, and one draw needn't show every extreme that they name: `key_tiles`: tiles have coordinates (frame layer, height, width) on a grid of 16 x 2 x 4, tile number (layer * 2 + height) * 4 + width. For each head and query tile, the first key_counts entries are distinct tiles that differ from the query tile by at most one in each coordinate, the query tile itself among them; the other entries repeat the query tile. In every head some tile lists its whole window.
All inputs are finite; a program needn't handle non-finite values.
Results may differ from a plain program's by a relative error of at most 0.0088.
Values may be sent and summed in bfloat16 or wider, within the bound.
A program may use at most 64 MiB of HBM per device.

v0:
```python
import jax
import jax.numpy as jnp
from jax import lax
from jax.sharding import PartitionSpec as P

TILE = 64
eps = 1e-06


def padded(block, sides, width):
    for axis, dim in sides:
        count = lax.axis_size(axis)
        forward = [(i, i + 1) for i in range(count - 1)]
        backward = [(target, source) for source, target in forward]
        low = lax.ppermute(
            lax.slice_in_dim(block, block.shape[dim] - width, None, axis=dim), axis, forward
        )
        high = lax.ppermute(lax.slice_in_dim(block, 0, width, axis=dim), axis, backward)
        block = jnp.concatenate([low, block, high], axis=dim)
    return block


def normed(rows, gain):
    stat = jnp.mean(rows * rows, axis=-1, keepdims=True)
    return rows * lax.rsqrt(stat + eps) * gain


def attend(query_rows, key_rows, value_rows, tile_ids, tile_counts, first_tile):
    heads = tile_ids.shape[0]
    slots = tile_ids.shape[2]
    head_dim = query_rows.shape[1] // heads
    query_tiles = query_rows.reshape(-1, TILE, heads, head_dim).transpose(2, 0, 1, 3)
    key_tiles = key_rows.reshape(-1, TILE, heads, head_dim).transpose(2, 0, 1, 3)
    value_tiles = value_rows.reshape(-1, TILE, heads, head_dim).transpose(2, 0, 1, 3)
    local_ids = tile_ids - first_tile
    picked_keys = jax.vmap(lambda lookup, indices: lookup[indices])(key_tiles, local_ids)
    picked_values = jax.vmap(lambda lookup, indices: lookup[indices])(value_tiles, local_ids)
    count_q = query_tiles.shape[1]
    picked_keys = picked_keys.reshape(heads, count_q, slots * TILE, head_dim)
    picked_values = picked_values.reshape(heads, count_q, slots * TILE, head_dim)
    scores = jnp.einsum(
        "hqtd,hqsd->hqts", query_tiles, picked_keys, preferred_element_type=jnp.float32
    ) * head_dim ** (-0.5)
    live = (jnp.arange(slots, dtype=jnp.int32)[None, None, :] < tile_counts[:, :, None]).astype(
        jnp.float32
    )
    live = jnp.repeat(live, TILE, axis=2)[:, :, None, :]
    weights = jnp.exp(scores) * live
    totals = jnp.sum(weights, axis=-1, keepdims=True)
    summed = (
        jnp.einsum(
            "hqts,hqsd->hqtd",
            weights.astype(jnp.bfloat16),
            picked_values,
            preferred_element_type=jnp.float32,
        )
        / totals
    )
    return summed.astype(jnp.bfloat16).transpose(1, 2, 0, 3).reshape(-1, heads * head_dim)


def body(frames, proj_weight, out_weight, query_gain, key_gain, key_tiles, key_counts):
    heads = key_tiles.shape[0]
    width = proj_weight.shape[2]
    head_dim = width // heads
    layer_tiles = key_tiles.shape[1]
    tok_count = frames.shape[0]
    columns = frames
    proj = jnp.einsum(
        "tn,cnw->ctw",
        columns,
        lax.all_gather(proj_weight, "ctx", axis=1, tiled=True),
        preferred_element_type=jnp.float32,
    )
    query_rows = normed(proj[0].reshape(-1, heads, head_dim), query_gain.reshape(heads, head_dim))
    key_rows = normed(proj[1].reshape(-1, heads, head_dim), key_gain.reshape(heads, head_dim))
    query_rows = query_rows.reshape(-1, width).astype(jnp.bfloat16)
    key_rows = key_rows.reshape(-1, width).astype(jnp.bfloat16)
    value_rows = proj[2].astype(jnp.bfloat16)
    paired = jnp.stack([key_rows, value_rows], axis=0)
    widened = padded(paired, (("ctx", 1),), tok_count)
    first_tile = (lax.axis_index("ctx") - 1) * layer_tiles
    attended = attend(query_rows, widened[0], widened[1], key_tiles, key_counts, first_tile)
    out_columns = lax.all_gather(out_weight, "ctx", axis=1, tiled=True)
    columns = out_columns
    mixed = lax.dot_general(
        lax.all_gather(attended, "dp", axis=1, tiled=True),
        columns,
        (((1,), (1,)), ((), ())),
        preferred_element_type=jnp.float32,
    )
    return mixed.astype(jnp.bfloat16)


def solution(mesh):
    placed = (
        P("ctx", None),
        P(None, "ctx", "dp"),
        P("dp", "ctx"),
        P("dp"),
        P("dp"),
        P("dp", "ctx", None),
        P("dp", "ctx"),
    )
    return jax.shard_map(
        body, mesh=mesh, in_specs=placed, out_specs=P("ctx", "dp"), check_vma=False
    )
```

profile of v0, /device:TPU:1, one launch (start us, length us, event | category | flops | bytes accessed | tf_op | source)
XLA Modules:
  0.0 201.2 jit_solution(7556137137856312792)
XLA Ops:
  6.5 0.0 all-gather.4.cloned.1.call-start
  6.5 2.1 %copy.12 = bf16[3,384,256]{1,2,0:T(8,128)(2,1)} copy(bf16[3,384,256]{2,1,0:T(8,128)(2,1)} %param.8) | data formatting | bytes 1179648 | tf_op args[1]
  8.7 0.0 all-gather.4.cloned.1.call-update
  8.7 0.0 all-gather.8.cloned.1.call-start
  8.8 0.7 all-gather.8.cloned.1.call-update
  9.5 0.0 all-gather.6.cloned.1.call-start
  9.5 0.7 fusion.23
  10.2 0.0 copy-start.1
  10.2 64.0 %all-gather.4.cloned.1.call-done = bf16[3,6144,256]{1,2,0:T(8,128)(2,1)} async-done(((bf16[3,384,256]{1,2,0:T(8,128)(2,1)}), bf16[3,6144,256]{1,2,0:T(8,128)(2,1)}) %all-gather.4.cloned.1.call-update) | async-done | bytes 9437200 | tf_op jit(solution)/shard_map/all_gather | solution.py:72
  74.2 9.5 %fusion.4 = f32[3,512,256]{1,2,0:T(8,128)S(1)} fusion(bf16[3,6144,256]{1,2,0:T(8,128)(2,1)} %all-gather.4.cloned.1.call-done, bf16[512,6144]{1,0:T(8,128)(2,1)} %param.7), kind=kOutput, calls=%fused_computation.9 | convolution fusion | flops 4831838208 | bytes 17301504 | tf_op jit(solution)/shard_map/tn,cnw->ctw/dot_general | solution.py:69
  83.7 0.0 copy-start.3
  83.8 0.0 copy-start.2
  83.8 0.1 reduce_sum.28
  83.9 0.0 copy-done.1
  83.9 0.2 slice_multiply_fusion.1
  84.1 0.1 pad_maximum_fusion.1
  84.2 1.9 collective-permute-start
  86.1 3.4 %collective-permute-start.1 = (bf16[2,512,256]{1,2,0:T(8,128)(2,1)S(1)}, bf16[2,512,256]{1,2,0:T(8,128)(2,1)}, u32[]{:S(2)}, u32[]{:S(2)}) collective-permute-start(bf16[2,512,256]{1,2,0:T(8,128)(2,1)S(1)} %pad_maximum_fusion.1), channel_id=1, source_target_pairs={{1,0},{2,1},{3,2},{4,3},{5,4},{6,5},{7,6},{8,7},{9,8},{10,9},{11,1... | collective-permute-start | bytes 1572872 | tf_op jit(solution)/shard_map/ppermute | solution.py:18
  89.5 0.0 copy-done.3
  89.5 0.1 fusion.24
  89.5 0.1 reshape.68
  89.6 0.1 broadcast_in_dim.5
  89.7 0.1 mul.100
  89.8 0.2 copy.13
  90.0 0.3 reshape_squeeze.10
  90.3 0.1 reduce_sum.27
  90.4 0.1 copy.14
  90.6 0.0 copy-done.2
  90.6 0.7 fusion.18
  91.3 3.3 %collective-permute-done = bf16[2,512,256]{1,2,0:T(8,128)(2,1)} collective-permute-done((bf16[2,512,256]{1,2,0:T(8,128)(2,1)S(1)}, bf16[2,512,256]{1,2,0:T(8,128)(2,1)}, u32[]{:S(2)}, u32[]{:S(2)}) %collective-permute-start) | collective-permute-done | bytes 524320 | tf_op jit(solution)/shard_map/ppermute | solution.py:15
  94.6 4.4 %collective-permute-done.1 = bf16[2,512,256]{1,2,0:T(8,128)(2,1)} collective-permute-done((bf16[2,512,256]{1,2,0:T(8,128)(2,1)S(1)}, bf16[2,512,256]{1,2,0:T(8,128)(2,1)}, u32[]{:S(2)}, u32[]{:S(2)}) %collective-permute-start.1) | collective-permute-done | bytes 524320 | tf_op jit(solution)/shard_map/ppermute | solution.py:18
  99.0 1.3 pad_maximum_fusion
  100.3 1.0 fusion.25
  101.3 0.9 reshape.88
  102.2 1.0 copy.16
  103.2 2.4 %reshape.89 = bf16[24,64,2,128]{1,0,3,2:T(8,128)(2,1)S(1)} reshape(bf16[1,1536,256]{1,2,0:T(8,128)(2,1)} %get-tuple-element.9) | data formatting | bytes 1572864 | tf_op jit(solution)/shard_map/reshape;squeeze | solution.py:34
  105.6 1.0 copy.19
  106.6 6.4 %gather_fusion = bf16[288,64,128]{2,1,0:T(8,128)(2,1)} fusion(bf16[2,24,64,128]{3,2,1,0:T(8,128)(2,1)S(1)} %bitcast.53, s32[288]{0:T(512)S(1)} %reshape.68), kind=kCustom, calls=%fused_computation | custom fusion | bytes 9439488 | tf_op jit(solution)/shard_map/vmap()/gather | solution.py:36
  113.0 6.3 %gather_fusion.1 = bf16[288,64,128]{2,1,0:T(8,128)(2,1)} fusion(bf16[2,24,64,128]{3,2,1,0:T(8,128)(2,1)S(1)} %bitcast.54, s32[288]{0:T(512)S(1)} %reshape.68), kind=kCustom, calls=%fused_computation.1 | custom fusion | bytes 9439488 | tf_op jit(solution)/shard_map/vmap()/gather | solution.py:37
  119.3 4.5 %fusion.26 = (f32[2,8,64]{2,1,0:T(8,128)S(1)}, bf16[2,8,64,1152]{3,2,1,0:T(8,128)(2,1)S(1)}) fusion(f32[2,8,1152]{2,1,0:T(8,128)S(1)} %mul.100, bf16[2,8,1152,128]{3,2,1,0:T(8,128)(2,1)} %bitcast.56, bf16[2,8,64,128]{3,0,2,1:T(2,128)(2,1)S(1)} %fusion.18), kind=kOutput, calls=%fused_computation.35 | convolution fusion | flops 306707456 | bytes 7417856 | tf_op jit(solution)/shard_map/hqtd,hqsd->hqts/dot_general | solution.py:41
  123.8 0.0 copy-done
  123.8 1.1 fusion.13
  124.9 0.3 copy.20
  125.2 0.7 copy.31
  125.9 0.0 all-gather.6.cloned.1.call-update
  126.0 0.0 all-gather.8.cloned.1.call-done
  126.0 62.4 %all-gather.6.cloned.1.call-done = bf16[512,4096]{1,0:T(8,128)(2,1)} async-done(((bf16[512,256]{1,0:T(8,128)(2,1)}), bf16[512,4096]{1,0:T(8,128)(2,1)}) %all-gather.6.cloned.1.call-update) | async-done | bytes 4194320 | tf_op jit(solution)/shard_map/all_gather | solution.py:87
  188.4 6.3 %convolution_convert_fusion = bf16[512,384]{1,0:T(8,128)(2,1)} fusion(bf16[512,4096]{1,0:T(8,128)(2,1)} %all-gather.6.cloned.1.call-done, bf16[384,4096]{1,0:T(8,128)(2,1)} %all-gather.8.cloned.1.call-done), kind=kOutput, calls=%fused_computation.10 | convolution fusion | flops 1610809344 | bytes 7733248 | tf_op jit(solution)/shard_map/dot_general | solution.py:86
  (5 shorter events, 0.1 us)
Async XLA Ops:
  6.5 67.6 %all-gather.4.cloned.1.call-start = ((), (), s32[]{:S(2)}) async-start(), calls=%async_computation | async-start | bytes 10027008 | tf_op jit(solution)/shard_map/all_gather | solution.py:72
  8.7 117.3 %all-gather.8.cloned.1.call-start = ((), (), s32[]{:S(2)}) async-start(), calls=%async_computation.2 | async-start | bytes 3342336 | tf_op jit(solution)/shard_map/all_gather | solution.py:84
  9.5 178.9 %all-gather.6.cloned.1.call-start = ((), (), s32[]{:S(2)}) async-start(), calls=%async_computation.1 | async-start | bytes 4456448 | tf_op jit(solution)/shard_map/all_gather | solution.py:87
  10.2 73.7 %copy-start.1 = (f32[256]{0:T(256)S(1)}, f32[256]{0:T(256)}, u32[]{:S(2)}) copy-start(f32[256]{0:T(256)} %param.11) | copy-start | bytes 3076
  83.7 5.8 %copy-start.3 = (s32[2,8]{1,0:T(2,128)S(1)}, s32[2,8]{1,0:T(2,128)}, u32[]{:S(2)}) copy-start(s32[2,8]{1,0:T(2,128)} %param.13) | copy-start | bytes 196
  83.8 6.8 %copy-start.2 = (f32[256]{0:T(256)S(1)}, f32[256]{0:T(256)}, u32[]{:S(2)}) copy-start(f32[256]{0:T(256)} %param.10) | copy-start | bytes 3076
  84.2 10.4 %collective-permute-start = (bf16[2,512,256]{1,2,0:T(8,128)(2,1)S(1)}, bf16[2,512,256]{1,2,0:T(8,128)(2,1)}, u32[]{:S(2)}, u32[]{:S(2)}) collective-permute-start(bf16[2,512,256]{1,2,0:T(8,128)(2,1)S(1)} %pad_maximum_fusion.1), channel_id=1, source_target_pairs={{0,1},{1,2},{2,3},{3,4},{4,5},{5,6},{6,7},{7,8},{8,9},{9,10},{10,1... | collective-permute-start | bytes 1572872 | tf_op jit(solution)/shard_map/ppermute | solution.py:15
  86.1 12.9 %collective-permute-start.1 = (bf16[2,512,256]{1,2,0:T(8,128)(2,1)S(1)}, bf16[2,512,256]{1,2,0:T(8,128)(2,1)}, u32[]{:S(2)}, u32[]{:S(2)}) collective-permute-start(bf16[2,512,256]{1,2,0:T(8,128)(2,1)S(1)} %pad_maximum_fusion.1), channel_id=1, source_target_pairs={{1,0},{2,1},{3,2},{4,3},{5,4},{6,5},{7,6},{8,7},{9,8},{10,9},{11,1... | collective-permute-start | bytes 1572872 | tf_op jit(solution)/shard_map/ppermute | solution.py:18
  119.3 4.5 %copy-start = (bf16[288,64,128]{2,1,0:T(8,128)(2,1)S(1)}, bf16[288,64,128]{2,1,0:T(8,128)(2,1)}, u32[]{:S(2)}) copy-start(bf16[288,64,128]{2,1,0:T(8,128)(2,1)} %gather_fusion.1) | copy-start | bytes 14155780
Sparse Core Ops, SparseCore 0:
  9.1 64.9 all-gather.3
  75.9 45.6 all-gather.7
  126.1 62.2 all-gather.5
where the time goes:
time: 202 us; the launch traced here: 201 us
  waiting for transfers between devices  135 us (67%)
  local copies, waits for them, and re-layouts  23 us (11%)
  matrix products  21.4 us (11%)
  between operations  13.3 us (7%)
  starting transfers between devices  5.36 us (3%)
  other arithmetic  3.22 us (2%)
    all_gather x1, waiting for transfers between devices, body(): lax.all_gather(proj_weight, 'ctx', axis=1, tiled=True)  64 us
    all_gather x1, waiting for transfers between devices, body(): lax.all_gather(attended, 'dp', axis=1, tiled=True)  62.4 us
    gather x3, local copies, waits for them, and re-layouts, attend(): lookup[indices]  12.7 us
    dot_general x1, matrix products, body(): jnp.einsum('tn,cnw->ctw', columns, lax.all_gather(proj_weight, 'ctx', axi...  9.52 us
    dot_general x1, matrix products, body(): lax.dot_general(lax.all_gather(attended, 'dp', axis=1, tiled=True), colum...  6.26 us
    dot_general x1, matrix products, attend(): jnp.einsum('hqtd,hqsd->hqts', query_tiles, picked_keys, preferred_element...  4.49 us
    ppermute x1, waiting for transfers between devices, padded(): lax.ppermute(lax.slice_in_dim(block, 0, width, axis=dim), axis, backward)  4.43 us
  transfers between devices with their start and end apart: 5, of which 4 were waited for; matrix products, arithmetic and copies ran while one was open for 19% of the time, Pallas kernels for 0%

commit v1 on v0

--- a/solution.py
+++ b/solution.py
@@ -66,12 +66,38 @@
     layer_tiles = key_tiles.shape[1]
     tok_count = frames.shape[0]
     columns = frames
-    proj = jnp.einsum(
+    devices, here, span = (lax.axis_size("ctx"), lax.axis_index("ctx"), proj_weight.shape[1])
+    upward = [(i_2, (i_2 + 1) % devices) for i_2 in range(devices)]
+    left = [(i_2, (i_2 - 1) % devices) for i_2 in range(devices)]
+    half = devices // 2
+    from_left = from_right = proj_weight
+    subtotal = jnp.einsum(
         "tn,cnw->ctw",
-        columns,
-        lax.all_gather(proj_weight, "ctx", axis=1, tiled=True),
+        lax.dynamic_slice_in_dim(columns, here * span, proj_weight.shape[1], axis=1),
+        proj_weight,
         preferred_element_type=jnp.float32,
     )
+    for turn in range(1, half + 1):
+        from_left = lax.ppermute(from_left, "ctx", upward)
+        if turn < devices - half:
+            from_right = lax.ppermute(from_right, "ctx", left)
+            subtotal = subtotal + jnp.einsum(
+                "tn,cnw->ctw",
+                lax.dynamic_slice_in_dim(
+                    columns, (here + turn) % devices * span, from_right.shape[1], axis=1
+                ),
+                from_right,
+                preferred_element_type=jnp.float32,
+            )
+        subtotal = subtotal + jnp.einsum(
+            "tn,cnw->ctw",
+            lax.dynamic_slice_in_dim(
+                columns, (here - turn) % devices * span, from_left.shape[1], axis=1
+            ),
+            from_left,
+            preferred_element_type=jnp.float32,
+        )
+    proj = subtotal
     query_rows = normed(proj[0].reshape(-1, heads, head_dim), query_gain.reshape(heads, head_dim))
     key_rows = normed(proj[1].reshape(-1, heads, head_dim), key_gain.reshape(heads, head_dim))
     query_rows = query_rows.reshape(-1, width).astype(jnp.bfloat16)

time: 202 us -> 228 us (1.13)
  starting transfers between devices: 5.36 us -> 62.4 us
  waiting for transfers between devices: 135 us -> 92.1 us
  matrix products: 21.4 us -> 32.8 us
    all_gather x1 -> x0, waiting for transfers between devices: 64 us -> none  [body(): lax.all_gather(proj_weight, 'ctx', axis=1, tiled=True)]
    ppermute x0 -> x15, starting transfers between devices: none -> 49.2 us  [the longest x7 33.3 us: body(): from_right = lax.ppermute(from_right, 'ctx', left)]
    ppermute x0 -> x15, waiting for transfers between devices: none -> 22.4 us  [the longest x8 21 us: body(): from_left = lax.ppermute(from_left, 'ctx', upward)]
    dot_general x1 -> x16, matrix products: 9.52 us -> 21 us  [the longest x8 11.6 us: body(): jnp.einsum('tn,cnw->ctw', lax.dynamic_slice_in_dim(columns, (here - turn)...]
    ppermute x1, starting transfers between devices: 3.35 us -> 11 us  [padded(): lax.ppermute(lax.slice_in_dim(block, 0, width, axis=dim), axis, backward)]
    all_gather x1, waiting for transfers between devices: 62.4 us -> 69.7 us  [body(): lax.all_gather(attended, 'dp', axis=1, tiled=True)]
    ppermute x1, waiting for transfers between devices: 4.43 us -> 0.01 us  [padded(): lax.ppermute(lax.slice_in_dim(block, 0, width, axis=dim), axis, backward)]
    ppermute x1, waiting for transfers between devices: 3.31 us -> 0.01 us  [padded(): lax.ppermute(lax.slice_in_dim(block, block.shape[dim] - width, None, axis...]
  transfers between devices with their start and end apart: 5 -> 19, of which waited for: 4 -> 9; matrix products, arithmetic and copies ran while one was open for 19% -> 22% of each run, Pallas kernels for 0% -> 0%
where the time goes in v1:
time: 228 us; the launch traced here: 227 us
  waiting for transfers between devices  92.1 us (40%)
  starting transfers between devices  62.4 us (27%)
  matrix products  32.8 us (14%)
  local copies, waits for them, and re-layouts  22.2 us (10%)
  between operations  14.1 us (6%)
  other arithmetic  3.32 us (1%)
    all_gather x1, waiting for transfers between devices, body(): lax.all_gather(attended, 'dp', axis=1, tiled=True)  69.7 us
    ppermute x7, starting transfers between devices, body(): from_right = lax.ppermute(from_right, 'ctx', left)  33.3 us
    ppermute x8, waiting for transfers between devices, body(): from_left = lax.ppermute(from_left, 'ctx', upward)  21 us
    ppermute x8, starting transfers between devices, body(): from_left = lax.ppermute(from_left, 'ctx', upward)  16 us
    gather x3, local copies, waits for them, and re-layouts, attend(): lookup[indices]  12.6 us
    dot_general x8, matrix products, body(): jnp.einsum('tn,cnw->ctw', lax.dynamic_slice_in_dim(columns, (here - turn)...  11.6 us
    ppermute x1, starting transfers between devices, padded(): lax.ppermute(lax.slice_in_dim(block, 0, width, axis=dim), axis, backward)  11 us
    dot_general x7, matrix products, body(): jnp.einsum('tn,cnw->ctw', lax.dynamic_slice_in_dim(columns, (here + turn)...  7.57 us
  transfers between devices with their start and end apart: 19, of which 9 were waited for; matrix products, arithmetic and copies ran while one was open for 22% of the time, Pallas kernels for 0%

profile of v1, /device:TPU:1, one launch (start us, length us, event | category | flops | bytes accessed | tf_op | source)
XLA Modules:
  0.0 227.0 jit_solution(13532312115436716568)
XLA Ops:
  6.5 1.4 copy.15
  7.9 3.0 %collective-permute-start.1 = (bf16[3,384,256]{1,2,0:T(8,128)(2,1)S(1)}, bf16[3,384,256]{1,2,0:T(8,128)(2,1)S(1)}, u32[]{:S(2)}, u32[]{:S(2)}) collective-permute-start(bf16[3,384,256]{1,2,0:T(8,128)(2,1)S(1)} %copy.15), channel_id=1, source_target_pairs={{0,1},{1,2},{2,3},{3,4},{4,5},{5,6},{6,7},{7,8},{8,9},{9,10},{10,1... | collective-permute-start | bytes 1769480 | tf_op jit(solution)/shard_map/ppermute | solution.py:81
  11.2 6.6 %collective-permute-done.1 = bf16[3,384,256]{1,2,0:T(8,128)(2,1)S(1)} collective-permute-done((bf16[3,384,256]{1,2,0:T(8,128)(2,1)S(1)}, bf16[3,384,256]{1,2,0:T(8,128)(2,1)S(1)}, u32[]{:S(2)}, u32[]{:S(2)}) %collective-permute-start.1) | collective-permute-done | bytes 589856 | tf_op jit(solution)/shard_map/ppermute | solution.py:81
  17.8 2.5 %collective-permute-start.3 = (bf16[3,384,256]{1,2,0:T(8,128)(2,1)S(1)}, bf16[3,384,256]{1,2,0:T(8,128)(2,1)S(1)}, u32[]{:S(2)}, u32[]{:S(2)}) collective-permute-start(bf16[3,384,256]{1,2,0:T(8,128)(2,1)S(1)} %collective-permute-done.1), channel_id=1, source_target_pairs={{0,1},{1,2},{2,3},{3,4},{4,5},{5,6},{6,7},{7,8},{8,9},{9,10},{10,1... | collective-permute-start | bytes 1769480 | tf_op jit(solution)/shard_map/ppermute | solution.py:81
  20.6 1.8 collective-permute-start.2
  22.3 4.8 %collective-permute-done.3 = bf16[3,384,256]{1,2,0:T(8,128)(2,1)S(1)} collective-permute-done((bf16[3,384,256]{1,2,0:T(8,128)(2,1)S(1)}, bf16[3,384,256]{1,2,0:T(8,128)(2,1)S(1)}, u32[]{:S(2)}, u32[]{:S(2)}) %collective-permute-start.3) | collective-permute-done | bytes 589856 | tf_op jit(solution)/shard_map/ppermute | solution.py:81
  27.1 2.5 %collective-permute-start.5 = (bf16[3,384,256]{1,2,0:T(8,128)(2,1)S(1)}, bf16[3,384,256]{1,2,0:T(8,128)(2,1)}, u32[]{:S(2)}, u32[]{:S(2)}) collective-permute-start(bf16[3,384,256]{1,2,0:T(8,128)(2,1)S(1)} %collective-permute-done.3), channel_id=1, source_target_pairs={{0,1},{1,2},{2,3},{3,4},{4,5},{5,6},{6,7},{7,8},{8,9},{9,10},{10,1... | collective-permute-start | bytes 1769480 | tf_op jit(solution)/shard_map/ppermute | solution.py:81
  30.2 2.8 %collective-permute-start.4 = (bf16[3,384,256]{1,2,0:T(8,128)(2,1)}, bf16[3,384,256]{1,2,0:T(8,128)(2,1)}, u32[]{:S(2)}, u32[]{:S(2)}) collective-permute-start(bf16[3,384,256]{1,2,0:T(8,128)(2,1)} %collective-permute-done.2), channel_id=1, source_target_pairs={{0,15},{1,0},{2,1},{3,2},{4,3},{5,4},{6,5},{7,6},{8,7},{9,8},{10,9... | collective-permute-start | bytes 1769480 | tf_op jit(solution)/shard_map/ppermute | solution.py:83
  32.9 1.8 fusion.42
  34.8 1.7 collective-permute-done.5
  36.4 2.6 %collective-permute-start.7 = (bf16[3,384,256]{1,2,0:T(8,128)(2,1)}, bf16[3,384,256]{1,2,0:T(8,128)(2,1)}, u32[]{:S(2)}, u32[]{:S(2)}) collective-permute-start(bf16[3,384,256]{1,2,0:T(8,128)(2,1)} %collective-permute-done.5), channel_id=1, source_target_pairs={{0,1},{1,2},{2,3},{3,4},{4,5},{5,6},{6,7},{7,8},{8,9},{9,10},{10,1... | collective-permute-start | bytes 1769480 | tf_op jit(solution)/shard_map/ppermute | solution.py:81
  39.3 1.9 fusion.38
  41.3 4.5 %collective-permute-start.6 = (bf16[3,384,256]{1,2,0:T(8,128)(2,1)}, bf16[3,384,256]{1,2,0:T(8,128)(2,1)S(1)}, u32[]{:S(2)}, u32[]{:S(2)}) collective-permute-start(bf16[3,384,256]{1,2,0:T(8,128)(2,1)} %collective-permute-done.4), channel_id=1, source_target_pairs={{0,15},{1,0},{2,1},{3,2},{4,3},{5,4},{6,5},{7,6},{8,7},{9,8},{10,9... | collective-permute-start | bytes 1769480 | tf_op jit(solution)/shard_map/ppermute | solution.py:83
  45.7 1.8 fusion.40
  47.5 0.7 collective-permute-done.7
  48.3 2.5 %collective-permute-start.9 = (bf16[3,384,256]{1,2,0:T(8,128)(2,1)}, bf16[3,384,256]{1,2,0:T(8,128)(2,1)S(1)}, u32[]{:S(2)}, u32[]{:S(2)}) collective-permute-start(bf16[3,384,256]{1,2,0:T(8,128)(2,1)} %collective-permute-done.7), channel_id=1, source_target_pairs={{0,1},{1,2},{2,3},{3,4},{4,5},{5,6},{6,7},{7,8},{8,9},{9,10},{10,1... | collective-permute-start | bytes 1769480 | tf_op jit(solution)/shard_map/ppermute | solution.py:81
  50.7 1.8 fusion.34
  52.5 1.7 fusion.36
  54.2 7.8 %collective-permute-start.8 = (bf16[3,384,256]{1,2,0:T(8,128)(2,1)S(1)}, bf16[3,384,256]{1,2,0:T(8,128)(2,1)S(1)}, u32[]{:S(2)}, u32[]{:S(2)}) collective-permute-start(bf16[3,384,256]{1,2,0:T(8,128)(2,1)S(1)} %collective-permute-done.6), channel_id=1, source_target_pairs={{0,15},{1,0},{2,1},{3,2},{4,3},{5,4},{6,5},{7,6},{8,7},{9,8},{10,9... | collective-permute-start | bytes 1769480 | tf_op jit(solution)/shard_map/ppermute | solution.py:83
  62.1 1.7 fusion.30
  63.8 1.2 collective-permute-start.11
  65.0 1.7 fusion.32
  66.6 1.7 fusion.26
  68.4 8.5 %collective-permute-start.10 = (bf16[3,384,256]{1,2,0:T(8,128)(2,1)S(1)}, bf16[3,384,256]{1,2,0:T(8,128)(2,1)S(1)}, u32[]{:S(2)}, u32[]{:S(2)}) collective-permute-start(bf16[3,384,256]{1,2,0:T(8,128)(2,1)S(1)} %collective-permute-done.8), channel_id=1, source_target_pairs={{0,15},{1,0},{2,1},{3,2},{4,3},{5,4},{6,5},{7,6},{8,7},{9,8},{10,9... | collective-permute-start | bytes 1769480 | tf_op jit(solution)/shard_map/ppermute | solution.py:83
  77.5 1.4 collective-permute-start.13
  79.5 0.6 fusion.24
  80.7 7.7 %collective-permute-start.12 = (bf16[3,384,256]{1,2,0:T(8,128)(2,1)S(1)}, bf16[3,384,256]{1,2,0:T(8,128)(2,1)S(1)}, u32[]{:S(2)}, u32[]{:S(2)}) collective-permute-start(bf16[3,384,256]{1,2,0:T(8,128)(2,1)S(1)} %collective-permute-done.10), channel_id=1, source_target_pairs={{0,15},{1,0},{2,1},{3,2},{4,3},{5,4},{6,5},{7,6},{8,7},{9,8},{10,9... | collective-permute-start | bytes 1769480 | tf_op jit(solution)/shard_map/ppermute | solution.py:83
  89.9 0.6 fusion.14
  90.5 0.6 fusion.16
  91.1 7.3 %collective-permute-done.14 = bf16[3,384,256]{1,2,0:T(8,128)(2,1)} collective-permute-done((bf16[3,384,256]{1,2,0:T(8,128)(2,1)S(1)}, bf16[3,384,256]{1,2,0:T(8,128)(2,1)}, u32[]{:S(2)}, u32[]{:S(2)}) %collective-permute-start.14) | collective-permute-done | bytes 589856 | tf_op jit(solution)/shard_map/ppermute | solution.py:81
  98.4 2.7 %add_bitcast_fusion = f32[3,512,256]{1,2,0:T(8,128)S(1)} fusion(f32[512,3,256]{0,2,1:T(8,128)S(1)} %fusion.14, f32[512,3,256]{0,2,1:T(8,128)S(1)} %fusion.16, f32[512,3,256]{0,2,1:T(8,128)S(1)} %fusion.18, f32[512,3,256]{0,2,1:T(8,128)S(1)} %fusion.20, f32[512,3,256]{0,2,1:T(8,128)S(1)} %fusion.22, f32[512,3,256]{0,2,1:T(8,128)S(1)} %fusion.24, ...), kind=kOutput, calls=%fused_computation.7 | convolution fusion | flops 307888128 | bytes 26148868 | tf_op jit(solution)/shard_map/tn,cnw->ctw/dot_general | solution.py:92
  101.5 0.8 pad_maximum_fusion.1
  102.3 2.2 collective-permute-start.15
  104.5 11.0 %collective-permute-start.16 = (bf16[2,512,256]{1,2,0:T(8,128)(2,1)}, bf16[2,512,256]{1,2,0:T(8,128)(2,1)}, u32[]{:S(2)}, u32[]{:S(2)}) collective-permute-start(bf16[2,512,256]{1,2,0:T(8,128)(2,1)} %pad_maximum_fusion.1), channel_id=1, source_target_pairs={{1,0},{2,1},{3,2},{4,3},{5,4},{6,5},{7,6},{8,7},{9,8},{10,9},{11,1... | collective-permute-start | bytes 1572872 | tf_op jit(solution)/shard_map/ppermute | solution.py:18
  116.6 0.7 fusion.60
  117.4 1.3 pad_maximum_fusion
  118.7 1.0 fusion.83
  119.7 0.9 reshape.103
  120.6 1.0 copy.20
  121.6 2.4 %reshape.104 = bf16[24,64,2,128]{1,0,3,2:T(8,128)(2,1)S(1)} reshape(bf16[1,1536,256]{1,2,0:T(8,128)(2,1)} %get-tuple-element.9) | data formatting | bytes 1572864 | tf_op jit(solution)/shard_map/reshape;squeeze | solution.py:34
  124.0 1.0 copy.23
  125.0 6.3 %gather_fusion = bf16[288,64,128]{2,1,0:T(8,128)(2,1)} fusion(bf16[2,24,64,128]{3,2,1,0:T(8,128)(2,1)S(1)} %bitcast.111, s32[288]{0:T(512)S(1)} %reshape.68), kind=kCustom, calls=%fused_computation | custom fusion | bytes 9439488 | tf_op jit(solution)/shard_map/vmap()/gather | solution.py:36
  131.3 6.2 %gather_fusion.1 = bf16[288,64,128]{2,1,0:T(8,128)(2,1)} fusion(bf16[2,24,64,128]{3,2,1,0:T(8,128)(2,1)S(1)} %bitcast.112, s32[288]{0:T(512)S(1)} %reshape.68), kind=kCustom, calls=%fused_computation.1 | custom fusion | bytes 9439488 | tf_op jit(solution)/shard_map/vmap()/gather | solution.py:37
  137.5 4.5 %fusion.84 = (f32[2,8,64]{2,1,0:T(8,128)S(1)}, bf16[2,8,64,1152]{3,2,1,0:T(8,128)(2,1)S(1)}) fusion(f32[2,8,1152]{2,1,0:T(8,128)S(1)} %mul.164, bf16[2,8,1152,128]{3,2,1,0:T(8,128)(2,1)} %bitcast.114, bf16[2,8,64,128]{3,0,2,1:T(2,128)(2,1)S(1)} %fusion.60), kind=kOutput, calls=%fused_computation.96 | convolution fusion | flops 306707456 | bytes 7417856 | tf_op jit(solution)/shard_map/hqtd,hqsd->hqts/dot_general | solution.py:41
  142.0 1.1 fusion.8
  143.4 0.7 copy.36
  144.2 69.7 %all-gather.3.cloned.1.call-done = bf16[512,4096]{1,0:T(8,128)(2,1)} async-done(((bf16[512,256]{1,0:T(8,128)(2,1)}), bf16[512,4096]{1,0:T(8,128)(2,1)}) %all-gather.3.cloned.1.call-update) | async-done | bytes 4194320 | tf_op jit(solution)/shard_map/all_gather | solution.py:113
  213.9 6.3 %convolution_convert_fusion = bf16[512,384]{1,0:T(8,128)(2,1)} fusion(bf16[512,4096]{1,0:T(8,128)(2,1)} %all-gather.3.cloned.1.call-done, bf16[384,4096]{1,0:T(8,128)(2,1)} %all-gather.5.cloned.1.call-done), kind=kOutput, calls=%fused_computation.8 | convolution fusion | flops 1610809344 | bytes 7733248 | tf_op jit(solution)/shard_map/dot_general | solution.py:112
  (57 shorter events, 6.1 us)
Async XLA Ops:
  6.5 32.5 %copy-start.5 = (s32[2,8,18]{2,1,0:T(8,128)S(1)}, s32[2,8,18]{2,1,0:T(8,128)}, u32[]{:S(2)}) copy-start(s32[2,8,18]{2,1,0:T(8,128)} %param.12) | copy-start | bytes 3460
  6.5 137.7 %all-gather.5.cloned.1.call-start = ((), (), s32[]{:S(2)}) async-start(), calls=%async_computation.1 | async-start | bytes 3342336 | tf_op jit(solution)/shard_map/all_gather | solution.py:110
  7.9 9.9 %collective-permute-start.1 = (bf16[3,384,256]{1,2,0:T(8,128)(2,1)S(1)}, bf16[3,384,256]{1,2,0:T(8,128)(2,1)S(1)}, u32[]{:S(2)}, u32[]{:S(2)}) collective-permute-start(bf16[3,384,256]{1,2,0:T(8,128)(2,1)S(1)} %copy.15), channel_id=1, source_target_pairs={{0,1},{1,2},{2,3},{3,4},{4,5},{5,6},{6,7},{7,8},{8,9},{9,10},{10,1... | collective-permute-start | bytes 1769480 | tf_op jit(solution)/shard_map/ppermute | solution.py:81
  11.0 9.6 %collective-permute-start = (bf16[3,384,256]{1,2,0:T(8,128)(2,1)S(1)}, bf16[3,384,256]{1,2,0:T(8,128)(2,1)S(1)}, u32[]{:S(2)}, u32[]{:S(2)}) collective-permute-start(bf16[3,384,256]{1,2,0:T(8,128)(2,1)S(1)} %copy.15), channel_id=1, source_target_pairs={{0,15},{1,0},{2,1},{3,2},{4,3},{5,4},{6,5},{7,6},{8,7},{9,8},{10,9... | collective-permute-start | bytes 1769480 | tf_op jit(solution)/shard_map/ppermute | solution.py:83
  17.8 9.3 %copy-start.4 = (bf16[3,384,256]{1,2,0:T(8,128)(2,1)}, bf16[3,384,256]{1,2,0:T(8,128)(2,1)S(1)}, u32[]{:S(2)}) copy-start(bf16[3,384,256]{1,2,0:T(8,128)(2,1)S(1)} %collective-permute-done.1) | copy-start | bytes 1769476
  17.8 9.3 %collective-permute-start.3 = (bf16[3,384,256]{1,2,0:T(8,128)(2,1)S(1)}, bf16[3,384,256]{1,2,0:T(8,128)(2,1)S(1)}, u32[]{:S(2)}, u32[]{:S(2)}) collective-permute-start(bf16[3,384,256]{1,2,0:T(8,128)(2,1)S(1)} %collective-permute-done.1), channel_id=1, source_target_pairs={{0,1},{1,2},{2,3},{3,4},{4,5},{5,6},{6,7},{7,8},{8,9},{9,10},{10,1... | collective-permute-start | bytes 1769480 | tf_op jit(solution)/shard_map/ppermute | solution.py:81
  20.6 9.6 %copy-start.3 = (bf16[3,384,256]{1,2,0:T(8,128)(2,1)}, bf16[3,384,256]{1,2,0:T(8,128)(2,1)S(1)}, u32[]{:S(2)}) copy-start(bf16[3,384,256]{1,2,0:T(8,128)(2,1)S(1)} %collective-permute-done) | copy-start | bytes 1769476
  20.6 9.6 %collective-permute-start.2 = (bf16[3,384,256]{1,2,0:T(8,128)(2,1)S(1)}, bf16[3,384,256]{1,2,0:T(8,128)(2,1)}, u32[]{:S(2)}, u32[]{:S(2)}) collective-permute-start(bf16[3,384,256]{1,2,0:T(8,128)(2,1)S(1)} %collective-permute-done), channel_id=1, source_target_pairs={{0,15},{1,0},{2,1},{3,2},{4,3},{5,4},{6,5},{7,6},{8,7},{9,8},{10,9... | collective-permute-start | bytes 1769480 | tf_op jit(solution)/shard_map/ppermute | solution.py:83
  27.1 12.2 %copy-start.2 = (bf16[3,384,256]{1,2,0:T(8,128)(2,1)}, bf16[3,384,256]{1,2,0:T(8,128)(2,1)S(1)}, u32[]{:S(2)}) copy-start(bf16[3,384,256]{1,2,0:T(8,128)(2,1)S(1)} %collective-permute-done.3) | copy-start | bytes 1769476
  27.1 9.3 %collective-permute-start.5 = (bf16[3,384,256]{1,2,0:T(8,128)(2,1)S(1)}, bf16[3,384,256]{1,2,0:T(8,128)(2,1)}, u32[]{:S(2)}, u32[]{:S(2)}) collective-permute-start(bf16[3,384,256]{1,2,0:T(8,128)(2,1)S(1)} %collective-permute-done.3), channel_id=1, source_target_pairs={{0,1},{1,2},{2,3},{3,4},{4,5},{5,6},{6,7},{7,8},{8,9},{9,10},{10,1... | collective-permute-start | bytes 1769480 | tf_op jit(solution)/shard_map/ppermute | solution.py:81
  29.6 184.3 %all-gather.3.cloned.1.call-start = ((), (), s32[]{:S(2)}) async-start(), calls=%async_computation | async-start | bytes 4456448 | tf_op jit(solution)/shard_map/all_gather | solution.py:113
  30.2 11.1 %collective-permute-start.4 = (bf16[3,384,256]{1,2,0:T(8,128)(2,1)}, bf16[3,384,256]{1,2,0:T(8,128)(2,1)}, u32[]{:S(2)}, u32[]{:S(2)}) collective-permute-start(bf16[3,384,256]{1,2,0:T(8,128)(2,1)} %collective-permute-done.2), channel_id=1, source_target_pairs={{0,15},{1,0},{2,1},{3,2},{4,3},{5,4},{6,5},{7,6},{8,7},{9,8},{10,9... | collective-permute-start | bytes 1769480 | tf_op jit(solution)/shard_map/ppermute | solution.py:83
  36.4 11.8 %collective-permute-start.7 = (bf16[3,384,256]{1,2,0:T(8,128)(2,1)}, bf16[3,384,256]{1,2,0:T(8,128)(2,1)}, u32[]{:S(2)}, u32[]{:S(2)}) collective-permute-start(bf16[3,384,256]{1,2,0:T(8,128)(2,1)} %collective-permute-done.5), channel_id=1, source_target_pairs={{0,1},{1,2},{2,3},{3,4},{4,5},{5,6},{6,7},{7,8},{8,9},{9,10},{10,1... | collective-permute-start | bytes 1769480 | tf_op jit(solution)/shard_map/ppermute | solution.py:81
  39.3 13.2 %copy-start = (bf16[512,6144]{1,0:T(8,128)(2,1)S(1)}, bf16[512,6144]{1,0:T(8,128)(2,1)}, u32[]{:S(2)}) copy-start(bf16[512,6144]{1,0:T(8,128)(2,1)} %param.7) | copy-start | bytes 18874372
  41.3 13.0 %collective-permute-start.6 = (bf16[3,384,256]{1,2,0:T(8,128)(2,1)}, bf16[3,384,256]{1,2,0:T(8,128)(2,1)S(1)}, u32[]{:S(2)}, u32[]{:S(2)}) collective-permute-start(bf16[3,384,256]{1,2,0:T(8,128)(2,1)} %collective-permute-done.4), channel_id=1, source_target_pairs={{0,15},{1,0},{2,1},{3,2},{4,3},{5,4},{6,5},{7,6},{8,7},{9,8},{10,9... | collective-permute-start | bytes 1769480 | tf_op jit(solution)/shard_map/ppermute | solution.py:83
  48.3 15.5 %collective-permute-start.9 = (bf16[3,384,256]{1,2,0:T(8,128)(2,1)}, bf16[3,384,256]{1,2,0:T(8,128)(2,1)S(1)}, u32[]{:S(2)}, u32[]{:S(2)}) collective-permute-start(bf16[3,384,256]{1,2,0:T(8,128)(2,1)} %collective-permute-done.7), channel_id=1, source_target_pairs={{0,1},{1,2},{2,3},{3,4},{4,5},{5,6},{6,7},{7,8},{8,9},{9,10},{10,1... | collective-permute-start | bytes 1769480 | tf_op jit(solution)/shard_map/ppermute | solution.py:81
  54.2 14.1 %collective-permute-start.8 = (bf16[3,384,256]{1,2,0:T(8,128)(2,1)S(1)}, bf16[3,384,256]{1,2,0:T(8,128)(2,1)S(1)}, u32[]{:S(2)}, u32[]{:S(2)}) collective-permute-start(bf16[3,384,256]{1,2,0:T(8,128)(2,1)S(1)} %collective-permute-done.6), channel_id=1, source_target_pairs={{0,15},{1,0},{2,1},{3,2},{4,3},{5,4},{6,5},{7,6},{8,7},{9,8},{10,9... | collective-permute-start | bytes 1769480 | tf_op jit(solution)/shard_map/ppermute | solution.py:83
  63.8 13.7 %collective-permute-start.11 = (bf16[3,384,256]{1,2,0:T(8,128)(2,1)S(1)}, bf16[3,384,256]{1,2,0:T(8,128)(2,1)S(1)}, u32[]{:S(2)}, u32[]{:S(2)}) collective-permute-start(bf16[3,384,256]{1,2,0:T(8,128)(2,1)S(1)} %collective-permute-done.9), channel_id=1, source_target_pairs={{0,1},{1,2},{2,3},{3,4},{4,5},{5,6},{6,7},{7,8},{8,9},{9,10},{10,1... | collective-permute-start | bytes 1769480 | tf_op jit(solution)/shard_map/ppermute | solution.py:81
  68.4 12.3 %collective-permute-start.10 = (bf16[3,384,256]{1,2,0:T(8,128)(2,1)S(1)}, bf16[3,384,256]{1,2,0:T(8,128)(2,1)S(1)}, u32[]{:S(2)}, u32[]{:S(2)}) collective-permute-start(bf16[3,384,256]{1,2,0:T(8,128)(2,1)S(1)} %collective-permute-done.8), channel_id=1, source_target_pairs={{0,15},{1,0},{2,1},{3,2},{4,3},{5,4},{6,5},{7,6},{8,7},{9,8},{10,9... | collective-permute-start | bytes 1769480 | tf_op jit(solution)/shard_map/ppermute | solution.py:83
  77.5 11.6 %collective-permute-start.13 = (bf16[3,384,256]{1,2,0:T(8,128)(2,1)S(1)}, bf16[3,384,256]{1,2,0:T(8,128)(2,1)S(1)}, u32[]{:S(2)}, u32[]{:S(2)}) collective-permute-start(bf16[3,384,256]{1,2,0:T(8,128)(2,1)S(1)} %collective-permute-done.11), channel_id=1, source_target_pairs={{0,1},{1,2},{2,3},{3,4},{4,5},{5,6},{6,7},{7,8},{8,9},{9,10},{10,1... | collective-permute-start | bytes 1769480 | tf_op jit(solution)/shard_map/ppermute | solution.py:81
  80.7 9.8 %collective-permute-start.12 = (bf16[3,384,256]{1,2,0:T(8,128)(2,1)S(1)}, bf16[3,384,256]{1,2,0:T(8,128)(2,1)S(1)}, u32[]{:S(2)}, u32[]{:S(2)}) collective-permute-start(bf16[3,384,256]{1,2,0:T(8,128)(2,1)S(1)} %collective-permute-done.10), channel_id=1, source_target_pairs={{0,15},{1,0},{2,1},{3,2},{4,3},{5,4},{6,5},{7,6},{8,7},{9,8},{10,9... | collective-permute-start | bytes 1769480 | tf_op jit(solution)/shard_map/ppermute | solution.py:83
  89.0 9.4 %collective-permute-start.14 = (bf16[3,384,256]{1,2,0:T(8,128)(2,1)S(1)}, bf16[3,384,256]{1,2,0:T(8,128)(2,1)}, u32[]{:S(2)}, u32[]{:S(2)}) collective-permute-start(bf16[3,384,256]{1,2,0:T(8,128)(2,1)S(1)} %collective-permute-done.13), channel_id=1, source_target_pairs={{0,1},{1,2},{2,3},{3,4},{4,5},{5,6},{6,7},{7,8},{8,9},{9,10},{10,1... | collective-permute-start | bytes 1769480 | tf_op jit(solution)/shard_map/ppermute | solution.py:81
  91.1 10.1 %copy-start.6 = (f32[256]{0:T(256)S(1)}, f32[256]{0:T(256)}, u32[]{:S(2)}) copy-start(f32[256]{0:T(256)} %param.11) | copy-start | bytes 3076
  101.1 14.4 %copy-start.8 = (s32[2,8]{1,0:T(2,128)S(1)}, s32[2,8]{1,0:T(2,128)}, u32[]{:S(2)}) copy-start(s32[2,8]{1,0:T(2,128)} %param.13) | copy-start | bytes 196
  101.5 15.1 %copy-start.7 = (f32[256]{0:T(256)S(1)}, f32[256]{0:T(256)}, u32[]{:S(2)}) copy-start(f32[256]{0:T(256)} %param.10) | copy-start | bytes 3076
  102.3 15.0 %collective-permute-start.15 = (bf16[2,512,256]{1,2,0:T(8,128)(2,1)}, bf16[2,512,256]{1,2,0:T(8,128)(2,1)}, u32[]{:S(2)}, u32[]{:S(2)}) collective-permute-start(bf16[2,512,256]{1,2,0:T(8,128)(2,1)} %pad_maximum_fusion.1), channel_id=1, source_target_pairs={{0,1},{1,2},{2,3},{3,4},{4,5},{5,6},{6,7},{7,8},{8,9},{9,10},{10,1... | collective-permute-start | bytes 1572872 | tf_op jit(solution)/shard_map/ppermute | solution.py:15
  104.5 12.8 %collective-permute-start.16 = (bf16[2,512,256]{1,2,0:T(8,128)(2,1)}, bf16[2,512,256]{1,2,0:T(8,128)(2,1)}, u32[]{:S(2)}, u32[]{:S(2)}) collective-permute-start(bf16[2,512,256]{1,2,0:T(8,128)(2,1)} %pad_maximum_fusion.1), channel_id=1, source_target_pairs={{1,0},{2,1},{3,2},{4,3},{5,4},{6,5},{7,6},{8,7},{9,8},{10,9},{11,1... | collective-permute-start | bytes 1572872 | tf_op jit(solution)/shard_map/ppermute | solution.py:18
  137.5 4.5 %copy-start.1 = (bf16[288,64,128]{2,1,0:T(8,128)(2,1)S(1)}, bf16[288,64,128]{2,1,0:T(8,128)(2,1)}, u32[]{:S(2)}) copy-start(bf16[288,64,128]{2,1,0:T(8,128)(2,1)} %gather_fusion.1) | copy-start | bytes 14155780
Sparse Core Ops, SparseCore 0:
  29.7 55.8 all-gather.4
  144.3 69.5 all-gather.2
